TPU v7x, 32 devices: a whole 2x2x4 slice. The times are simulated.
32 devices in a mesh: wide: 4 (over z), narrow: 8 (over y, x, core).
Axes of the slice: x: 2, y: 2, z: 4, core: 2. Of those that a mesh axis runs over, the one named last changes fastest.
Arguments:
- hidden: bfloat16 [512, 4096], P('wide', 'narrow'), may hold values from -6 to 6
- norm_gain: float32 [4096], replicated, may hold values from 0.1 to 1.9
- w_query: bfloat16 [4096, 8192], P(None, 'narrow'), may hold values from -0.09375 to 0.09375
- w_keyval: bfloat16 [4096, 1024], P('narrow'), may hold values from -0.09375 to 0.09375
- query_gain: float32 [128], replicated, may hold values from 0.5 to 4
- key_gain: float32 [128], replicated, may hold values from 0.5 to 4
- cache_keys: bfloat16 [32, 16384, 512], P('wide', 'narrow'), may hold values from -300 to 300
- cache_values: bfloat16 [32, 16384, 512], P('wide', 'narrow'), may hold values from -6 to 6
- cache_lengths: int32 [32], P('wide'), may hold values from 1 to 16384
- owner_rank: int32 [32], P('wide'), may hold values from 0 to 3, as said below
- draft_mask: int32 [32, 16, 16], P('wide'), may hold values from 0 to 1, as said below
- w_output: bfloat16 [8192, 4096], P('narrow'), may hold values from -0.0625 to 0.0625
Outputs:
- projected: bfloat16 [512, 4096], P('wide', 'narrow')
Inputs may be any that keep to these rules, and one draw needn't show every extreme that they name: `owner_rank`: in each aligned block of 8 requests every index of wide is named exactly 2 times. Row t of a request marks the ancestors of draft token t in a tree of draft tokens and t itself: draft_mask[r, t, t] = 1 and draft_mask[r, t, u] = 0 for u > t.
All inputs are finite; a program needn't handle non-finite values.
Results may differ from a plain program's by a relative error of at most 0.007.
The roundings to bfloat16 on the way count: a program that leaves them out, or rounds other values in their place, can miss the bound.
Values may be sent and summed in bfloat16 or wider, within the bound.
A program may use at most 192 MiB of HBM per device.

v0:
```python
import functools
import math

import jax
import jax.numpy as jnp
from jax import lax
from jax.experimental import pallas as pl
from jax.experimental.pallas import tpu as pltpu
from jax.sharding import PartitionSpec as P

HQ = 64
KVH = 4
HD = 128
DRAFT = 16

epsilon = 1e-06
masked_fill = -1e30
SCALE = math.log2(math.e) / math.sqrt(HD)


def rms_norm(values, gain_row):
    return (
        values * lax.rsqrt(jnp.mean(values * values, axis=-1, keepdims=True) + epsilon) * gain_row
    )


def attend_kernel(narrow_count, lengths_ref, base_ref, q_ref, k_ref, v_ref, o_ref, stats_ref):
    span = k_ref.shape[1]
    rows = q_ref.shape[2]
    per_key = narrow_count // KVH
    request = pl.program_id(0)
    remaining = lengths_ref[request] - base_ref[0]
    ones = jnp.ones((span, HD), jnp.bfloat16)
    lanes = lax.broadcasted_iota(jnp.int32, (per_key * rows, HD), 1)

    def body(masked):
        stats = jnp.zeros((per_key * rows, HD), jnp.float32)
        for k in range(KVH):
            q = q_ref[k * per_key : (k + 1) * per_key, 0].reshape(per_key * rows, HD)
            keys = k_ref[0, :, k * HD : (k + 1) * HD]
            values = v_ref[0, :, k * HD : (k + 1) * HD]
            scores = lax.dot_general(
                q, keys, (((1,), (1,)), ((), ())), preferred_element_type=jnp.float32
            )
            if masked:
                live = lax.broadcasted_iota(jnp.int32, scores.shape, 1) < remaining
                scores = jnp.where(live, scores, masked_fill)
            top = jnp.max(scores, axis=1, keepdims=True) * SCALE
            weights = jnp.exp2(scores * SCALE - top).astype(jnp.bfloat16)
            both = jnp.dot(
                weights,
                jnp.concatenate([values, ones], axis=1),
                preferred_element_type=jnp.float32,
            )
            o_ref[k * per_key : (k + 1) * per_key, 0] = (
                both[:, :HD].astype(jnp.bfloat16).reshape(per_key, rows, HD)
            )
            stats = jnp.where(lanes == 2 * k, top, stats)
            stats = jnp.where(lanes == 2 * k + 1, both[:, HD:], stats)
        turned = stats.T
        for k in range(KVH):
            for i in range(per_key):
                for which in range(2):
                    stats_ref[k * per_key + i, which, pl.ds(request, 1), :] = turned[
                        2 * k + which : 2 * k + which + 1, i * rows : (i + 1) * rows
                    ]

    @pl.when(remaining >= span)
    def _():
        body(False)

    @pl.when((remaining > 0) & (remaining < span))
    def _():
        body(True)

    @pl.when(remaining <= 0)
    def _():
        o_ref[...] = jnp.zeros_like(o_ref)
        for d in range(narrow_count):
            stats_ref[d, 0, pl.ds(request, 1), :] = jnp.full((1, rows), masked_fill, jnp.float32)
            stats_ref[d, 1, pl.ds(request, 1), :] = jnp.zeros((1, rows), jnp.float32)


def attend(queries, cache_keys, cache_values, lengths, base):
    narrow_count, requests, rows, _ = queries.shape
    span = cache_keys.shape[1]
    q_spec = pl.BlockSpec((narrow_count, 1, rows, HD), lambda r, *_: (0, r, 0, 0))
    kv_spec = pl.BlockSpec((1, span, KVH * HD), lambda r, *_: (r, 0, 0))
    return pl.pallas_call(
        functools.partial(attend_kernel, narrow_count),
        grid_spec=pltpu.PrefetchScalarGridSpec(
            num_scalar_prefetch=2,
            grid=(requests,),
            in_specs=[q_spec, kv_spec, kv_spec],
            out_specs=[
                q_spec,
                pl.BlockSpec(
                    (narrow_count, 2, requests, rows), lambda r, *_: (0, 0, 0, 0)
                ),
            ],
        ),
        out_shape=[
            jax.ShapeDtypeStruct(queries.shape, jnp.bfloat16),
            jax.ShapeDtypeStruct((narrow_count, 2, requests, rows), jnp.float32),
        ],
        compiler_params=pltpu.CompilerParams(vmem_limit_bytes=48 * 1024 * 1024),
        cost_estimate=pl.CostEstimate(
            flops=4 * requests * narrow_count * rows * span * HD,
            bytes_accessed=4 * requests * span * KVH * HD,
            transcendentals=requests * narrow_count * rows * span,
        ),
    )(lengths, base, queries, cache_keys, cache_values)


MIB = 1024 * 1024


def remote(src, dst, send_sem, recv_sem, wide, narrow):
    return pltpu.make_async_remote_copy(
        src_ref=src,
        dst_ref=dst,
        send_sem=send_sem,
        recv_sem=recv_sem,
        device_id=(wide, narrow),
        device_id_type=pl.DeviceIdType.MESH,
    )


def greet(peers):
    barrier = pltpu.get_barrier_semaphore()
    for peer in peers:
        pl.semaphore_signal(
            barrier, inc=1, device_id=peer, device_id_type=pl.DeviceIdType.MESH
        )
    pl.semaphore_wait(barrier, len(peers))


def slot_rows(owner_ref, token_ids, per_pair):
    requests = owner_ref.shape[0]
    owners = [owner_ref[r] for r in range(requests)]
    rows = jnp.zeros_like(token_ids)
    for r in range(requests):
        place = owners[r] * per_pair
        for earlier in range(r):
            place = place + jnp.where(owners[earlier] == owners[r], 1, 0)
        rows = jnp.where(token_ids // DRAFT == r, place * DRAFT + token_ids % DRAFT, rows)
    return rows


def gather_chips(buffer, send_sem, recv_sem, wide, me, chips, between=None):
    chip, core = me // 2, me % 2
    mate = chip * 2 + 1 - core
    sends = []

    def send(block, target, slot):
        copy = remote(
            buffer.at[block],
            buffer.at[block],
            send_sem.at[slot],
            recv_sem.at[block],
            wide,
            target,
        )
        copy.start()
        sends.append(copy)

    for off in range(1, chips):
        send(me, lax.rem(chip + off, chips) * 2 + core, off)
    send(me, mate, 0)
    if between is not None:
        between()

    def arrived(block):
        remote(
            buffer.at[block], buffer.at[block], send_sem.at[0], recv_sem.at[block], wide, mate
        ).wait_recv()

    for off in range(1, chips):
        block = lax.rem(chip - off + chips, chips) * 2 + core
        arrived(block)
        send(block, mate, chips - 1 + off)
    arrived(mate)
    for off in range(1, chips):
        arrived(lax.rem(chip - off + chips, chips) * 2 + 1 - core)
    for copy in sends:
        copy.wait_send()


def front_kernel(
    wide_count,
    narrow_count,
    owner_ref,
    hidden_ref,
    mask_ref,
    gain_ref,
    query_gain_ref,
    wq_hbm,
    wkv_ref,
    q_out,
    own_out,
    mask_out,
    kv_out,
    wq,
    staged,
    landed,
    gathered,
    q_all,
    kv_part,
    kv_land,
    kv_pair,
    wq_sem,
    a_send,
    a_recv,
    g_send,
    g_recv,
    q_send,
    q_recv,
    k_send,
    k_recv,
):
    wide, me = lax.axis_index("wide"), lax.axis_index("narrow")
    chips = narrow_count // 2
    chip, core = me // 2, me % 2
    mate = chip * 2 + 1 - core
    tokens, features = hidden_ref.shape
    requests = tokens // DRAFT
    part = tokens // wide_count
    per_head = HQ // narrow_count
    per_key = narrow_count // KVH

    load = pltpu.make_async_copy(wq_hbm, wq, wq_sem)
    load.start()
    peers = [(lax.rem(wide + off, wide_count), me) for off in range(1, wide_count)]
    peers += [(wide, lax.rem(chip + off, chips) * 2 + core) for off in range(1, chips)]
    peers += [(wide, mate)]
    greet(peers)

    target = slot_rows(
        owner_ref, lax.broadcasted_iota(jnp.int32, (tokens, tokens), 1), part // DRAFT
    )
    chosen = lax.broadcasted_iota(jnp.int32, (tokens, tokens), 0) == target
    chosen = jnp.where(chosen, 1.0, 0.0).astype(jnp.bfloat16)
    staged[:, :features] = jnp.dot(
        chosen, hidden_ref[...], preferred_element_type=jnp.float32
    ).astype(jnp.bfloat16)
    staged[:, features:] = jnp.dot(
        chosen, mask_ref[...], preferred_element_type=jnp.float32
    ).astype(jnp.bfloat16)

    sends = []
    for off in range(1, wide_count):
        there = lax.rem(wide + off, wide_count)
        copy = remote(
            staged.at[pl.ds(pl.multiple_of(there * part, part), part)],
            landed.at[wide],
            a_send.at[off],
            a_recv.at[wide],
            there,
            me,
        )
        copy.start()
        sends.append(copy)
    landed[wide] = staged[pl.ds(pl.multiple_of(wide * part, part), part)]
    for off in range(1, wide_count):
        there = lax.rem(wide - off + wide_count, wide_count)
        remote(
            landed.at[there], landed.at[there], a_send.at[0], a_recv.at[there], there, me
        ).wait_recv()
    rows = landed[...].reshape(tokens, features + tokens)
    gathered[me] = rows[:, :features]
    mask_out[...] = rows[:, features:]
    gather_chips(gathered, g_send, g_recv, wide, me, chips)
    for copy in sends:
        copy.wait_send()

    squares = jnp.zeros((tokens, 1), jnp.float32)
    for j in range(narrow_count):
        block = gathered[j].astype(jnp.float32)
        squares += jnp.sum(block * block, axis=1, keepdims=True)
    factor = lax.rsqrt(squares * (1.0 / (narrow_count * features)) + epsilon)

    def normed(j):
        return (gathered[j].astype(jnp.float32) * factor * gain_ref[j]).astype(jnp.bfloat16)

    keyval = jnp.dot(normed(me), wkv_ref[...], preferred_element_type=jnp.float32)
    for c in range(chips):
        k = c * 2 // per_key
        kv_part[c, :, :HD] = keyval[:, k * HD : (k + 1) * HD]
        kv_part[c, :, HD:] = keyval[:, (KVH + k) * HD : (KVH + k + 1) * HD]
    kv_sends = []
    for off in range(1, chips):
        there = lax.rem(chip + off, chips)
        copy = remote(
            kv_part.at[there],
            kv_land.at[chip],
            k_send.at[off],
            k_recv.at[chip],
            wide,
            there * 2 + core,
        )
        copy.start()
        kv_sends.append(copy)

    load.wait()
    total = jnp.zeros((tokens, per_head * HD), jnp.float32)
    for j in range(narrow_count):
        total += jnp.dot(
            normed(j),
            wq[j * features : (j + 1) * features, :],
            preferred_element_type=jnp.float32,
        )
    for h in range(per_head):
        one = rms_norm(total[:, h * HD : (h + 1) * HD], query_gain_ref[...]).astype(jnp.bfloat16)
        q_all[me, :, h * DRAFT : (h + 1) * DRAFT, :] = one.reshape(requests, DRAFT, HD)

    def exchange_kv():
        summed = kv_part[chip]
        for off in range(1, chips):
            there = lax.rem(chip - off + chips, chips)
            remote(
                kv_land.at[there],
                kv_land.at[there],
                k_send.at[0],
                k_recv.at[there],
                wide,
                there * 2 + core,
            ).wait_recv()
            summed = summed + kv_land[there]
        kv_pair[0] = summed
        copy = remote(
            kv_pair.at[0], kv_pair.at[1], k_send.at[0], k_recv.at[chips], wide, mate
        )
        copy.start()
        kv_sends.append(copy)

    gather_chips(q_all, q_send, q_recv, wide, me, chips, exchange_kv)
    q_out[...] = q_all[...]
    own_out[...] = q_all[me]
    remote(
        kv_pair.at[0], kv_pair.at[1], k_send.at[0], k_recv.at[chips], wide, mate
    ).wait_recv()
    kv_out[...] = kv_pair[0] + kv_pair[1]
    for copy in kv_sends:
        copy.wait_send()


def back_kernel(
    wide_count,
    narrow_count,
    owner_ref,
    q_ref,
    mask_ref,
    kv_ref,
    key_gain_ref,
    o_hbm,
    stats_hbm,
    wo_hbm,
    out_ref,
    wo,
    o_land,
    s_land,
    att,
    mate_part,
    mate_land,
    chip_part,
    chip_land,
    y,
    y_land,
    wo_sem,
    own_sem,
    o_send,
    o_recv,
    s_send,
    s_recv,
    m_send,
    m_recv,
    c_send,
    c_recv,
    y_send,
    y_recv,
):
    wide, me = lax.axis_index("wide"), lax.axis_index("narrow")
    chips = narrow_count // 2
    chip, core = me // 2, me % 2
    mate = chip * 2 + 1 - core
    requests, rows, _ = q_ref.shape
    tokens, features = out_ref.shape
    part = tokens // wide_count
    per_head = rows // DRAFT

    load = pltpu.make_async_copy(wo_hbm, wo, wo_sem)
    load.start()
    peers = [(lax.rem(wide + off, wide_count), me) for off in range(1, wide_count)]
    peers += [(wide, lax.rem(me + off, narrow_count)) for off in range(1, narrow_count)]
    greet(peers)

    sends = []
    for off in range(1, narrow_count):
        there = lax.rem(me + off, narrow_count)
        for copy in (
            remote(
                stats_hbm.at[there], s_land.at[me], s_send.at[off], s_recv.at[me], wide, there
            ),
            remote(o_hbm.at[there], o_land.at[me], o_send.at[off], o_recv.at[me], wide, there),
        ):
            copy.start()
            sends.append(copy)
    own = [
        pltpu.make_async_copy(stats_hbm.at[me], s_land.at[me], own_sem.at[0]),
        pltpu.make_async_copy(o_hbm.at[me], o_land.at[me], own_sem.at[1]),
    ]
    for copy in own:
        copy.start()

    draft_keys = rms_norm(kv_ref[:, :HD], key_gain_ref[...]).astype(jnp.bfloat16)
    draft_values = kv_ref[:, HD:].astype(jnp.bfloat16)
    request_of = lax.broadcasted_iota(jnp.int32, (rows, tokens), 1) // DRAFT
    drafts = []
    for r in range(requests):
        scores = (
            lax.dot_general(
                q_ref[r], draft_keys, (((1,), (1,)), ((), ())), preferred_element_type=jnp.float32
            )
            * SCALE
        )
        mask = mask_ref[r * DRAFT : (r + 1) * DRAFT, :].astype(jnp.float32)
        seen = (jnp.concatenate([mask] * per_head, axis=0) == 1.0) & (request_of == r)
        scores = jnp.where(seen, scores, masked_fill)
        top = jnp.max(scores, axis=1, keepdims=True)
        weights = jnp.where(seen, jnp.exp2(scores - top), 0.0)
        total = jnp.sum(weights, axis=1, keepdims=True)
        summed = jnp.dot(
            weights.astype(jnp.bfloat16), draft_values, preferred_element_type=jnp.float32
        )
        drafts.append((top, total, summed))

    for copy in own:
        copy.wait()
    for off in range(1, narrow_count):
        there = lax.rem(me - off + narrow_count, narrow_count)
        remote(
            s_land.at[there], s_land.at[there], s_send.at[0], s_recv.at[there], wide, there
        ).wait_recv()
        remote(
            o_land.at[there], o_land.at[there], o_send.at[0], o_recv.at[there], wide, there
        ).wait_recv()

    tops = s_land[0, 0]
    for j in range(1, narrow_count):
        tops = jnp.maximum(tops, s_land[j, 0])
    scaling = [jnp.exp2(s_land[j, 0] - tops) for j in range(narrow_count)]
    totals = scaling[0] * s_land[0, 1]
    for j in range(1, narrow_count):
        totals = totals + scaling[j] * s_land[j, 1]
    listed = jnp.concatenate(scaling + [tops, totals], axis=0)
    filled = -(-listed.shape[0] // 128) * 128
    if filled > listed.shape[0]:
        listed = jnp.concatenate(
            [listed, jnp.zeros((filled - listed.shape[0], rows), jnp.float32)], axis=0
        )
    turned = listed.T

    def column(which, r):
        place = which * requests + r
        return turned[:, place : place + 1]

    for r in range(requests):
        draft_top, draft_total, joined = drafts[r]
        cache_top = column(narrow_count, r)
        top = jnp.maximum(cache_top, draft_top)
        cache_scale, draft_scale = jnp.exp2(cache_top - top), jnp.exp2(draft_top - top)
        summed = column(0, r) * o_land[0, r].astype(jnp.float32)
        for j in range(1, narrow_count):
            summed = summed + column(j, r) * o_land[j, r].astype(jnp.float32)
        total = column(narrow_count + 1, r) * cache_scale + draft_total * draft_scale
        value = ((summed * cache_scale + joined * draft_scale) / total).astype(jnp.bfloat16)
        for h in range(per_head):
            att[r * DRAFT : (r + 1) * DRAFT, h * HD : (h + 1) * HD] = value[
                h * DRAFT : (h + 1) * DRAFT
            ]

    load.wait()

    def terms(device):
        place = pl.ds(pl.multiple_of(device * features, features), features)
        return jnp.dot(att[...], wo[:, place], preferred_element_type=jnp.float32)

    for step in range(1, chips + 1):
        there = lax.rem(chip + step, chips)
        mate_part[there] = terms(there * 2 + 1 - core).astype(jnp.bfloat16)
        copy = remote(
            mate_part.at[there],
            mate_land.at[there],
            m_send.at[there],
            m_recv.at[there],
            wide,
            mate,
        )
        copy.start()
        sends.append(copy)
    summed = None
    for step in range(1, chips + 1):
        there = lax.rem(chip + step, chips)
        value = terms(there * 2 + core)
        remote(
            mate_land.at[there], mate_land.at[there], m_send.at[0], m_recv.at[there], wide, mate
        ).wait_recv()
        value = value + mate_land[there].astype(jnp.float32)
        if step < chips:
            chip_part[there] = value.astype(jnp.bfloat16)
            copy = remote(
                chip_part.at[there],
                chip_land.at[chip],
                c_send.at[there],
                c_recv.at[chip],
                wide,
                there * 2 + core,
            )
            copy.start()
            sends.append(copy)
        else:
            summed = value
    for off in range(1, chips):
        there = lax.rem(chip - off + chips, chips)
        remote(
            chip_land.at[there],
            chip_land.at[there],
            c_send.at[0],
            c_recv.at[there],
            wide,
            there * 2 + core,
        ).wait_recv()
        summed = summed + chip_land[there].astype(jnp.float32)
    y[...] = summed.astype(jnp.bfloat16)

    for off in range(1, wide_count):
        there = lax.rem(wide + off, wide_count)
        copy = remote(
            y.at[pl.ds(pl.multiple_of(there * part, part), part)],
            y_land.at[wide],
            y_send.at[off],
            y_recv.at[wide],
            there,
            me,
        )
        copy.start()
        sends.append(copy)
    y_land[wide] = y[pl.ds(pl.multiple_of(wide * part, part), part)]
    source = slot_rows(
        owner_ref, lax.broadcasted_iota(jnp.int32, (tokens, tokens), 0), part // DRAFT
    )
    chosen = lax.broadcasted_iota(jnp.int32, (tokens, tokens), 1) == source
    chosen = jnp.where(chosen, 1.0, 0.0).astype(jnp.bfloat16)
    for off in range(1, wide_count):
        there = lax.rem(wide - off + wide_count, wide_count)
        remote(
            y_land.at[there], y_land.at[there], y_send.at[0], y_recv.at[there], there, me
        ).wait_recv()
    out_ref[...] = jnp.dot(
        chosen, y_land[...].reshape(tokens, features), preferred_element_type=jnp.float32
    ).astype(jnp.bfloat16)
    for copy in sends:
        copy.wait_send()


def local(
    hidden,
    norm_gain,
    w_query,
    w_keyval,
    query_gain,
    key_gain,
    cache_keys,
    cache_values,
    cache_lengths,
    owner_rank,
    draft_mask,
    w_output,
):
    narrow_count = lax.axis_size("narrow")
    wide_count = lax.axis_size("wide")
    tokens, features = hidden.shape
    requests = tokens // DRAFT
    per_head = HQ // narrow_count
    span = cache_keys.shape[1]
    part = tokens // wide_count
    chips = narrow_count // 2
    rows = per_head * DRAFT
    vmem = pl.BlockSpec(memory_space=pltpu.VMEM)
    smem = pl.BlockSpec(memory_space=pltpu.SMEM)
    anywhere = pl.BlockSpec(memory_space=pl.ANY)
    dma = pltpu.SemaphoreType.DMA
    bf16, f32 = jnp.bfloat16, jnp.float32

    mask_rows = jnp.tile(draft_mask.reshape(tokens, DRAFT).astype(bf16), (1, tokens // DRAFT))
    all_queries, own_queries, owned_mask, keyval = pl.pallas_call(
        functools.partial(front_kernel, wide_count, narrow_count),
        out_shape=[
            jax.ShapeDtypeStruct((narrow_count, requests, rows, HD), bf16),
            jax.ShapeDtypeStruct((requests, rows, HD), bf16),
            jax.ShapeDtypeStruct((tokens, tokens), bf16),
            jax.ShapeDtypeStruct((tokens, 2 * HD), f32),
        ],
        in_specs=[smem, vmem, vmem, vmem, vmem, anywhere, vmem],
        out_specs=[vmem] * 4,
        scratch_shapes=[
            pltpu.VMEM(w_query.shape, bf16),
            pltpu.VMEM((tokens, features + tokens), bf16),
            pltpu.VMEM((wide_count, part, features + tokens), bf16),
            pltpu.VMEM((narrow_count, tokens, features), bf16),
            pltpu.VMEM((narrow_count, requests, rows, HD), bf16),
            pltpu.VMEM((chips, tokens, 2 * HD), f32),
            pltpu.VMEM((chips, tokens, 2 * HD), f32),
            pltpu.VMEM((2, tokens, 2 * HD), f32),
            dma,
            dma((wide_count,)),
            dma((wide_count,)),
            dma((narrow_count,)),
            dma((narrow_count,)),
            dma((narrow_count,)),
            dma((narrow_count,)),
            dma((chips,)),
            dma((chips + 1,)),
        ],
        compiler_params=pltpu.CompilerParams(
            collective_id=0, has_side_effects=True, vmem_limit_bytes=40 * MIB
        ),
    )(
        owner_rank,
        hidden,
        mask_rows,
        norm_gain.reshape(narrow_count, 1, features),
        query_gain.reshape(1, HD),
        w_query,
        w_keyval,
    )

    base = (lax.axis_index("narrow") * span).astype(jnp.int32).reshape(1)
    partial, stats = attend(all_queries, cache_keys, cache_values, cache_lengths, base)

    return pl.pallas_call(
        functools.partial(back_kernel, wide_count, narrow_count),
        out_shape=jax.ShapeDtypeStruct((tokens, features), bf16),
        in_specs=[smem, vmem, vmem, vmem, vmem, anywhere, anywhere, anywhere],
        out_specs=vmem,
        scratch_shapes=[
            pltpu.VMEM(w_output.shape, bf16),
            pltpu.VMEM((narrow_count, requests, rows, HD), bf16),
            pltpu.VMEM((narrow_count, 2, requests, rows), f32),
            pltpu.VMEM((tokens, per_head * HD), bf16),
            pltpu.VMEM((chips, tokens, features), bf16),
            pltpu.VMEM((chips, tokens, features), bf16),
            pltpu.VMEM((chips, tokens, features), bf16),
            pltpu.VMEM((chips, tokens, features), bf16),
            pltpu.VMEM((tokens, features), bf16),
            pltpu.VMEM((wide_count, part, features), bf16),
            dma,
            dma((2,)),
            dma((narrow_count,)),
            dma((narrow_count,)),
            dma((narrow_count,)),
            dma((narrow_count,)),
            dma((chips,)),
            dma((chips,)),
            dma((chips,)),
            dma((chips,)),
            dma((wide_count,)),
            dma((wide_count,)),
        ],
        compiler_params=pltpu.CompilerParams(
            collective_id=1, has_side_effects=True, vmem_limit_bytes=40 * MIB
        ),
    )(
        owner_rank,
        own_queries,
        owned_mask,
        keyval,
        key_gain.reshape(1, HD),
        partial,
        stats,
        w_output,
    )


def solution(mesh):
    in_specs = (
        P("wide", "narrow"),
        P(),
        P(None, "narrow"),
        P("narrow", None),
        P(),
        P(),
        P("wide", "narrow", None),
        P("wide", "narrow", None),
        P("wide"),
        P("wide"),
        P("wide", None, None),
        P("narrow", None),
    )
    out_specs = P("wide", "narrow")
    return jax.shard_map(local, mesh=mesh, in_specs=in_specs, out_specs=out_specs, check_vma=False)
```

profile of v0, /device:TPU:0, one launch (start us, length us, event | category | flops | bytes accessed | tf_op | source)
XLA Modules:
  0.0 125.3 jit_solution(9867390892106120373)
XLA Ops:
  0.0 0.0 copy-start.7
  0.0 0.9 convert_element_type.10
  0.9 0.1 copy.13
  0.9 0.1 copy.14.mask_ref
  1.1 0.0 copy-start
  1.1 3.4 %copy-done = bf16[4096,1024]{1,0:T(8,128)(2,1)S(1)} copy-done((bf16[4096,1024]{1,0:T(8,128)(2,1)S(1)}, bf16[4096,1024]{1,0:T(8,128)(2,1)}, u32[]{:S(2)}) %copy-start) | copy-done | bytes 8388632
  4.5 0.0 copy-start.1
  4.5 1.2 copy-done.1
  5.7 0.0 copy-start.2
  5.7 0.9 copy-done.2
  6.6 0.0 copy-start.3
  6.6 0.7 copy-done.3
  7.3 0.0 copy-start.4
  7.3 0.7 copy-done.4
  8.0 0.0 copy-start.6
  8.0 0.7 copy-done.6
  8.6 0.0 slice-start
  8.6 40.7 %shard_map.118 = (bf16[8,8,128,128]{3,2,1,0:T(8,128)(2,1)S(1)}, bf16[8,128,128]{2,1,0:T(8,128)(2,1)S(1)}, bf16[128,128]{1,0:T(8,128)(2,1)S(1)}, f32[128,256]{1,0:T(8,128)S(1)}) custom-call(s32[8]{0:T(128)S(1)} %copy-done.4, bf16[128,512]{1,0:T(8,128)(2,1)S(1)} %copy-done.2, bf16[128,128]{1,0:T(8,128)(2,1)S(1)} %copy.14.mask_ref, f32[8,1,512]{2,1,0:T(1,128)S(1)} %bitcast.8, ...), custom_call_target="tpu_custom_call" | custom-call | tf_op jit(solution)/shard_map/pallas_call | solution.py:596
  49.4 0.0 copy-done.7
  49.4 0.0 slice-start.1
  49.4 0.0 copy-start.5
  49.4 0.0 copy-start.8
  49.4 30.3 %shard_map.119 = (bf16[8,8,128,128]{3,2,1,0:T(8,128)(2,1)S(1)}, f32[8,2,8,128]{3,2,1,0:T(8,128)S(1)}) custom-call(s32[8]{0:T(128)S(1)} %copy-done.7, s32[1]{0:T(128)} %bitcast.5.base_ref, bf16[8,8,128,128]{3,2,1,0:T(8,128)(2,1)S(1)} %get-tuple-element.14.q_ref, bf16[8,2048,512]{2,1,0:T(8,128)(2,1)} %k_ref.1, bf16[8,2048,512]{2,1,0:T(8,128)(2,1)} %v_ref.1), custom_call_target="tpu_custom_call" | custom-call | flops 8589934592 | bytes 33554432 | tf_op jit(solution)/shard_map/pallas_call | solution.py:89
  79.8 0.0 slice-done
  79.8 0.0 slice-done.1
  79.8 0.0 copy-done.5
  79.8 0.0 copy-done.8
  79.8 44.9 %shard_map.120 = bf16[128,512]{1,0:T(8,128)(2,1)S(1)} custom-call(s32[8]{0:T(128)S(1)} %copy-done.5, bf16[8,128,128]{2,1,0:T(8,128)(2,1)S(1)} %get-tuple-element.11.q_ref, bf16[128,128]{1,0:T(8,128)(2,1)S(1)} %get-tuple-element.12.mask_ref, f32[128,256]{1,0:T(8,128)S(1)} %get-tuple-element.13.kv_ref, f32[1,128]{1,0:T(1,128)S(1)} %bitcast.10, ...), custom_call_target="tpu_custom_call" | custom-call | tf_op jit(solution)/shard_map/pallas_call | solution.py:641
  124.7 0.7 copy.16
  (2 shorter events, 0.0 us)
Async XLA Ops:
  0.0 49.4 %copy-start.7 = (s32[8]{0:T(128)S(1)}, s32[8]{0:T(128)}, u32[]{:S(2)}) copy-start(s32[8]{0:T(128)} %lengths_ref.1) | copy-start | bytes 100
  1.1 3.4 %copy-start = (bf16[4096,1024]{1,0:T(8,128)(2,1)S(1)}, bf16[4096,1024]{1,0:T(8,128)(2,1)}, u32[]{:S(2)}) copy-start(bf16[4096,1024]{1,0:T(8,128)(2,1)} %wq_hbm.1) | copy-start | bytes 25165828
  4.5 1.2 copy-start.1
  5.7 0.9 copy-start.2
  6.6 0.7 copy-start.3
  7.3 0.7 copy-start.4
  8.0 0.7 copy-start.6
  8.6 71.1 %slice-start = ((s8[8388608]{0:T(1024)(128)(4,1)}), s8[4194304]{0:T(1024)(128)(4,1)S(1)}, s32[]{:S(2)}) async-start(s8[8388608]{0:T(1024)(128)(4,1)} %bitcast.6), calls=%async_computation | async-start | bytes 8388608
  49.4 30.4 %slice-start.1 = ((s8[8388608]{0:T(1024)(128)(4,1)}), s8[4194304]{0:T(1024)(128)(4,1)S(1)}, s32[]{:S(2)}) async-start(s8[8388608]{0:T(1024)(128)(4,1)} %bitcast.6), calls=%async_computation.1 | async-start | bytes 8388608
  49.4 30.4 %copy-start.5 = (s32[8]{0:T(128)S(1)}, s32[8]{0:T(128)}, u32[]{:S(2)}) copy-start(s32[8]{0:T(128)} %owner_ref.3) | copy-start | bytes 100
  49.4 30.4 %copy-start.8 = (f32[128]{0:T(128)S(1)}, f32[128]{0:T(128)}, u32[]{:S(2)}) copy-start(f32[128]{0:T(128)} %param.17) | copy-start | bytes 1540
where the time goes:
time: 126 us; the launch traced here: 125 us
  Pallas kernels  116 us (92%)
  local copies, waits for them, and re-layouts  8.43 us (7%)
    pallas_call x1, Pallas kernels, local(): pl.pallas_call(functools.partial(back_kernel, wide_count, narrow_count),...  44.9 us
    pallas_call x1, Pallas kernels, local(): pl.pallas_call(functools.partial(front_kernel, wide_count, narrow_count),...  40.7 us
    pallas_call x1, Pallas kernels, attend(): pl.pallas_call(functools.partial(attend_kernel, narrow_count), grid_spec=...  30.3 us
    unnamed x23, local copies, waits for them, and re-layouts  8.23 us

commit v1 on v0

--- a/solution.py
+++ b/solution.py
@@ -24,95 +24,8 @@
     )
 
 
-def attend_kernel(narrow_count, lengths_ref, base_ref, q_ref, k_ref, v_ref, o_ref, stats_ref):
-    span = k_ref.shape[1]
-    rows = q_ref.shape[2]
-    per_key = narrow_count // KVH
-    request = pl.program_id(0)
-    remaining = lengths_ref[request] - base_ref[0]
-    ones = jnp.ones((span, HD), jnp.bfloat16)
-    lanes = lax.broadcasted_iota(jnp.int32, (per_key * rows, HD), 1)
-
-    def body(masked):
-        stats = jnp.zeros((per_key * rows, HD), jnp.float32)
-        for k in range(KVH):
-            q = q_ref[k * per_key : (k + 1) * per_key, 0].reshape(per_key * rows, HD)
-            keys = k_ref[0, :, k * HD : (k + 1) * HD]
-            values = v_ref[0, :, k * HD : (k + 1) * HD]
-            scores = lax.dot_general(
-                q, keys, (((1,), (1,)), ((), ())), preferred_element_type=jnp.float32
-            )
-            if masked:
-                live = lax.broadcasted_iota(jnp.int32, scores.shape, 1) < remaining
-                scores = jnp.where(live, scores, masked_fill)
-            top = jnp.max(scores, axis=1, keepdims=True) * SCALE
-            weights = jnp.exp2(scores * SCALE - top).astype(jnp.bfloat16)
-            both = jnp.dot(
-                weights,
-                jnp.concatenate([values, ones], axis=1),
-                preferred_element_type=jnp.float32,
-            )
-            o_ref[k * per_key : (k + 1) * per_key, 0] = (
-                both[:, :HD].astype(jnp.bfloat16).reshape(per_key, rows, HD)
-            )
-            stats = jnp.where(lanes == 2 * k, top, stats)
-            stats = jnp.where(lanes == 2 * k + 1, both[:, HD:], stats)
-        turned = stats.T
-        for k in range(KVH):
-            for i in range(per_key):
-                for which in range(2):
-                    stats_ref[k * per_key + i, which, pl.ds(request, 1), :] = turned[
-                        2 * k + which : 2 * k + which + 1, i * rows : (i + 1) * rows
-                    ]
-
-    @pl.when(remaining >= span)
-    def _():
-        body(False)
-
-    @pl.when((remaining > 0) & (remaining < span))
-    def _():
-        body(True)
-
-    @pl.when(remaining <= 0)
-    def _():
-        o_ref[...] = jnp.zeros_like(o_ref)
-        for d in range(narrow_count):
-            stats_ref[d, 0, pl.ds(request, 1), :] = jnp.full((1, rows), masked_fill, jnp.float32)
-            stats_ref[d, 1, pl.ds(request, 1), :] = jnp.zeros((1, rows), jnp.float32)
-
-
-def attend(queries, cache_keys, cache_values, lengths, base):
-    narrow_count, requests, rows, _ = queries.shape
-    span = cache_keys.shape[1]
-    q_spec = pl.BlockSpec((narrow_count, 1, rows, HD), lambda r, *_: (0, r, 0, 0))
-    kv_spec = pl.BlockSpec((1, span, KVH * HD), lambda r, *_: (r, 0, 0))
-    return pl.pallas_call(
-        functools.partial(attend_kernel, narrow_count),
-        grid_spec=pltpu.PrefetchScalarGridSpec(
-            num_scalar_prefetch=2,
-            grid=(requests,),
-            in_specs=[q_spec, kv_spec, kv_spec],
-            out_specs=[
-                q_spec,
-                pl.BlockSpec(
-                    (narrow_count, 2, requests, rows), lambda r, *_: (0, 0, 0, 0)
-                ),
-            ],
-        ),
-        out_shape=[
-            jax.ShapeDtypeStruct(queries.shape, jnp.bfloat16),
-            jax.ShapeDtypeStruct((narrow_count, 2, requests, rows), jnp.float32),
-        ],
-        compiler_params=pltpu.CompilerParams(vmem_limit_bytes=48 * 1024 * 1024),
-        cost_estimate=pl.CostEstimate(
-            flops=4 * requests * narrow_count * rows * span * HD,
-            bytes_accessed=4 * requests * span * KVH * HD,
-            transcendentals=requests * narrow_count * rows * span,
-        ),
-    )(lengths, base, queries, cache_keys, cache_values)
-
-
 MIB = 1024 * 1024
+PAIR = 2
 
 
 def remote(src, dst, send_sem, recv_sem, wide, narrow):
@@ -190,16 +103,20 @@
     wide_count,
     narrow_count,
     owner_ref,
+    hidden_hbm,
+    mask_hbm,
+    gain_hbm,
+    query_gain_hbm,
+    wkv_hbm,
+    wq_hbm,
+    q_out,
+    mask_out,
+    kv_out,
     hidden_ref,
     mask_ref,
     gain_ref,
     query_gain_ref,
-    wq_hbm,
     wkv_ref,
-    q_out,
-    own_out,
-    mask_out,
-    kv_out,
     wq,
     staged,
     landed,
@@ -208,6 +125,7 @@
     kv_part,
     kv_land,
     kv_pair,
+    small_sem,
     wq_sem,
     a_send,
     a_recv,
@@ -228,12 +146,27 @@
     per_head = HQ // narrow_count
     per_key = narrow_count // KVH
 
+    small = [
+        pltpu.make_async_copy(source, held, small_sem.at[i])
+        for i, (source, held) in enumerate(
+            [
+                (hidden_hbm, hidden_ref),
+                (mask_hbm, mask_ref),
+                (gain_hbm, gain_ref),
+                (query_gain_hbm, query_gain_ref),
+                (wkv_hbm, wkv_ref),
+            ]
+        )
+    ]
     load = pltpu.make_async_copy(wq_hbm, wq, wq_sem)
-    load.start()
+    for copy in small + [load]:
+        copy.start()
     peers = [(lax.rem(wide + off, wide_count), me) for off in range(1, wide_count)]
     peers += [(wide, lax.rem(chip + off, chips) * 2 + core) for off in range(1, chips)]
     peers += [(wide, mate)]
     greet(peers)
+    for copy in small[:2]:
+        copy.wait()
 
     target = slot_rows(
         owner_ref, lax.broadcasted_iota(jnp.int32, (tokens, tokens), 1), part // DRAFT
@@ -273,6 +206,8 @@
     for copy in sends:
         copy.wait_send()
 
+    for copy in small[2:]:
+        copy.wait()
     squares = jnp.zeros((tokens, 1), jnp.float32)
     for j in range(narrow_count):
         block = gathered[j].astype(jnp.float32)
@@ -335,7 +270,6 @@
 
     gather_chips(q_all, q_send, q_recv, wide, me, chips, exchange_kv)
     q_out[...] = q_all[...]
-    own_out[...] = q_all[me]
     remote(
         kv_pair.at[0], kv_pair.at[1], k_send.at[0], k_recv.at[chips], wide, mate
     ).wait_recv()
@@ -348,15 +282,19 @@
     wide_count,
     narrow_count,
     owner_ref,
+    lengths_ref,
     q_ref,
     mask_ref,
     kv_ref,
     key_gain_ref,
-    o_hbm,
-    stats_hbm,
+    k_hbm,
+    v_hbm,
     wo_hbm,
     out_ref,
     wo,
+    o_part,
+    s_part,
+    columns,
     o_land,
     s_land,
     att,
@@ -367,7 +305,6 @@
     y,
     y_land,
     wo_sem,
-    own_sem,
     o_send,
     o_recv,
     s_send,
@@ -383,7 +320,7 @@
     chips = narrow_count // 2
     chip, core = me // 2, me % 2
     mate = chip * 2 + 1 - core
-    requests, rows, _ = q_ref.shape
+    _, requests, rows, _ = q_ref.shape
     tokens, features = out_ref.shape
     part = tokens // wide_count
     per_head = rows // DRAFT
@@ -395,22 +332,69 @@
     greet(peers)
 
     sends = []
-    for off in range(1, narrow_count):
-        there = lax.rem(me + off, narrow_count)
+    span = k_hbm.shape[1]
+    per_key = narrow_count // KVH
+    my_key = me // per_key
+    lanes = lax.broadcasted_iota(jnp.int32, (per_key * rows, HD), 1)
+    ones = jnp.ones((span, HD), jnp.bfloat16)
+
+    def send(there):
         for copy in (
             remote(
-                stats_hbm.at[there], s_land.at[me], s_send.at[off], s_recv.at[me], wide, there
+                s_part.at[there], s_land.at[me], s_send.at[there], s_recv.at[me], wide, there
             ),
-            remote(o_hbm.at[there], o_land.at[me], o_send.at[off], o_recv.at[me], wide, there),
+            remote(
+                o_part.at[there], o_land.at[me], o_send.at[there], o_recv.at[me], wide, there
+            ),
         ):
             copy.start()
             sends.append(copy)
-    own = [
-        pltpu.make_async_copy(stats_hbm.at[me], s_land.at[me], own_sem.at[0]),
-        pltpu.make_async_copy(o_hbm.at[me], o_land.at[me], own_sem.at[1]),
-    ]
-    for copy in own:
-        copy.start()
+
+    for step in range(1, KVH + 1):
+        key = lax.rem(my_key + step, KVH)
+        first = key * per_key
+
+        def body(k_ref, v_ref, first=first):
+            for i in range(PAIR):
+                r = pl.program_id(0) * PAIR + i
+                q = jnp.concatenate([q_ref[first + d, r] for d in range(per_key)], axis=0)
+                scores = lax.dot_general(
+                    q, k_ref[i], (((1,), (1,)), ((), ())), preferred_element_type=jnp.float32
+                )
+                remaining = lengths_ref[r] - me * span
+                live = lax.broadcasted_iota(jnp.int32, scores.shape, 1) < remaining
+                scores = jnp.where(live, scores, masked_fill)
+                top = jnp.max(scores, axis=1, keepdims=True) * SCALE
+                weights = jnp.exp2(scores * SCALE - top).astype(jnp.bfloat16)
+                both = jnp.dot(
+                    weights,
+                    jnp.concatenate([v_ref[i], ones], axis=1),
+                    preferred_element_type=jnp.float32,
+                )
+                for d in range(per_key):
+                    o_part[first + d, r] = both[d * rows : (d + 1) * rows, :HD].astype(
+                        jnp.bfloat16
+                    )
+                held = jnp.where(lanes == r, top, columns[...])
+                columns[...] = jnp.where(lanes == requests + r, both[:, HD:], held)
+
+        columns[...] = jnp.zeros_like(columns)
+        spec = pl.BlockSpec((PAIR, span, HD), lambda r, key=key: (r, 0, key))
+        pltpu.emit_pipeline(body, grid=(requests // PAIR,), in_specs=[spec, spec])(k_hbm, v_hbm)
+        turned = columns[...].T
+        for d in range(per_key):
+            for which in range(2):
+                s_part[first + d, which] = turned[
+                    which * requests : (which + 1) * requests, d * rows : (d + 1) * rows
+                ]
+        if step < KVH:
+            for d in range(per_key):
+                send(first + d)
+        else:
+            for off in range(1, per_key):
+                send(first + lax.rem(me - first + off, per_key))
+    s_land[me] = s_part[me]
+    o_land[me] = o_part[me]
 
     draft_keys = rms_norm(kv_ref[:, :HD], key_gain_ref[...]).astype(jnp.bfloat16)
     draft_values = kv_ref[:, HD:].astype(jnp.bfloat16)
@@ -419,7 +403,7 @@
     for r in range(requests):
         scores = (
             lax.dot_general(
-                q_ref[r], draft_keys, (((1,), (1,)), ((), ())), preferred_element_type=jnp.float32
+                q_ref[me, r], draft_keys, (((1,), (1,)), ((), ())), preferred_element_type=jnp.float32
             )
             * SCALE
         )
@@ -434,8 +418,6 @@
         )
         drafts.append((top, total, summed))
 
-    for copy in own:
-        copy.wait()
     for off in range(1, narrow_count):
         there = lax.rem(me - off + narrow_count, narrow_count)
         remote(
@@ -582,7 +564,6 @@
     tokens, features = hidden.shape
     requests = tokens // DRAFT
     per_head = HQ // narrow_count
-    span = cache_keys.shape[1]
     part = tokens // wide_count
     chips = narrow_count // 2
     rows = per_head * DRAFT
@@ -593,17 +574,21 @@
     bf16, f32 = jnp.bfloat16, jnp.float32
 
     mask_rows = jnp.tile(draft_mask.reshape(tokens, DRAFT).astype(bf16), (1, tokens // DRAFT))
-    all_queries, own_queries, owned_mask, keyval = pl.pallas_call(
+    all_queries, owned_mask, keyval = pl.pallas_call(
         functools.partial(front_kernel, wide_count, narrow_count),
         out_shape=[
             jax.ShapeDtypeStruct((narrow_count, requests, rows, HD), bf16),
-            jax.ShapeDtypeStruct((requests, rows, HD), bf16),
             jax.ShapeDtypeStruct((tokens, tokens), bf16),
             jax.ShapeDtypeStruct((tokens, 2 * HD), f32),
         ],
-        in_specs=[smem, vmem, vmem, vmem, vmem, anywhere, vmem],
-        out_specs=[vmem] * 4,
+        in_specs=[smem] + [anywhere] * 6,
+        out_specs=[vmem] * 3,
         scratch_shapes=[
+            pltpu.VMEM(hidden.shape, bf16),
+            pltpu.VMEM((tokens, tokens), bf16),
+            pltpu.VMEM((narrow_count, 1, features), f32),
+            pltpu.VMEM((1, HD), f32),
+            pltpu.VMEM(w_keyval.shape, bf16),
             pltpu.VMEM(w_query.shape, bf16),
             pltpu.VMEM((tokens, features + tokens), bf16),
             pltpu.VMEM((wide_count, part, features + tokens), bf16),
@@ -612,6 +597,7 @@
             pltpu.VMEM((chips, tokens, 2 * HD), f32),
             pltpu.VMEM((chips, tokens, 2 * HD), f32),
             pltpu.VMEM((2, tokens, 2 * HD), f32),
+            dma((5,)),
             dma,
             dma((wide_count,)),
             dma((wide_count,)),
@@ -623,7 +609,7 @@
             dma((chips + 1,)),
         ],
         compiler_params=pltpu.CompilerParams(
-            collective_id=0, has_side_effects=True, vmem_limit_bytes=40 * MIB
+            collective_id=0, has_side_effects=True, vmem_limit_bytes=56 * MIB
         ),
     )(
         owner_rank,
@@ -631,20 +617,20 @@
         mask_rows,
         norm_gain.reshape(narrow_count, 1, features),
         query_gain.reshape(1, HD),
+        w_keyval,
         w_query,
-        w_keyval,
     )
-
-    base = (lax.axis_index("narrow") * span).astype(jnp.int32).reshape(1)
-    partial, stats = attend(all_queries, cache_keys, cache_values, cache_lengths, base)
 
     return pl.pallas_call(
         functools.partial(back_kernel, wide_count, narrow_count),
         out_shape=jax.ShapeDtypeStruct((tokens, features), bf16),
-        in_specs=[smem, vmem, vmem, vmem, vmem, anywhere, anywhere, anywhere],
+        in_specs=[smem, smem, vmem, vmem, vmem, vmem, anywhere, anywhere, anywhere],
         out_specs=vmem,
         scratch_shapes=[
             pltpu.VMEM(w_output.shape, bf16),
+            pltpu.VMEM((narrow_count, requests, rows, HD), bf16),
+            pltpu.VMEM((narrow_count, 2, requests, rows), f32),
+            pltpu.VMEM((narrow_count // KVH * rows, HD), f32),
             pltpu.VMEM((narrow_count, requests, rows, HD), bf16),
             pltpu.VMEM((narrow_count, 2, requests, rows), f32),
             pltpu.VMEM((tokens, per_head * HD), bf16),
@@ -655,7 +641,6 @@
             pltpu.VMEM((tokens, features), bf16),
             pltpu.VMEM((wide_count, part, features), bf16),
             dma,
-            dma((2,)),
             dma((narrow_count,)),
             dma((narrow_count,)),
             dma((narrow_count,)),
@@ -668,16 +653,17 @@
             dma((wide_count,)),
         ],
         compiler_params=pltpu.CompilerParams(
-            collective_id=1, has_side_effects=True, vmem_limit_bytes=40 * MIB
+            collective_id=1, has_side_effects=True, vmem_limit_bytes=56 * MIB
         ),
     )(
         owner_rank,
-        own_queries,
+        cache_lengths,
+        all_queries,
         owned_mask,
         keyval,
         key_gain.reshape(1, HD),
-        partial,
-        stats,
+        cache_keys,
+        cache_values,
         w_output,
     )
 

time: 126 us -> 112 us (0.89)
  Pallas kernels: 116 us -> 108 us
  local copies, waits for them, and re-layouts: 8.43 us -> 2.39 us
    pallas_call x1 -> x0, Pallas kernels: 30.3 us -> none  [attend(): pl.pallas_call(functools.partial(attend_kernel, narrow_count), grid_spec=...]
    pallas_call x1, Pallas kernels: 44.9 us -> 66.9 us  [local(): pl.pallas_call(functools.partial(back_kernel, wide_count, narrow_count),...]
    unnamed x23 -> x1, local copies, waits for them, and re-layouts: 8.23 us -> 1.57 us
where the time goes in v1:
time: 112 us; the launch traced here: 111 us
  Pallas kernels  108 us (96%)
  local copies, waits for them, and re-layouts  2.39 us (2%)
    pallas_call x1, Pallas kernels, local(): pl.pallas_call(functools.partial(back_kernel, wide_count, narrow_count),...  66.9 us
    pallas_call x1, Pallas kernels, local(): pl.pallas_call(functools.partial(front_kernel, wide_count, narrow_count),...  41.3 us

profile of v1, /device:TPU:0, one launch (start us, length us, event | category | flops | bytes accessed | tf_op | source)
XLA Modules:
  0.0 111.4 jit_solution(7716220883748371536)
XLA Ops:
  0.0 0.8 convert_element_type.10
  0.8 0.1 copy.13
  0.9 0.7 copy.14.mask_hbm
  1.7 41.3 %shard_map.118 = (bf16[8,8,128,128]{3,2,1,0:T(8,128)(2,1)}, bf16[128,128]{1,0:T(8,128)(2,1)}, f32[128,256]{1,0:T(8,128)}) custom-call(s32[8]{0:T(128)} %owner_ref.3, bf16[128,512]{1,0:T(8,128)(2,1)} %hidden_hbm.1, bf16[128,128]{1,0:T(8,128)(2,1)} %copy.14.mask_hbm, f32[8,1,512]{2,1,0:T(1,128)} %bitcast.7, f32[1,128]{1,0:T(1,128)} %bitcast.8, ...), custom_call_target="tpu_custom_call" | custom-call | tf_op jit(solution)/shard_map/pallas_call | solution.py:577
  42.9 66.9 %shard_map.119 = bf16[128,512]{1,0:T(8,128)(2,1)} custom-call(s32[8]{0:T(128)} %owner_ref.3, s32[8]{0:T(128)} %lengths_ref.1, bf16[8,8,128,128]{3,2,1,0:T(8,128)(2,1)} %get-tuple-element.8.q_ref, bf16[128,128]{1,0:T(8,128)(2,1)} %get-tuple-element.9.mask_ref, f32[128,256]{1,0:T(8,128)} %get-tuple-element.10.kv_ref, f32[1,128]{1,0:T(1,128)} %bitcast.9, ...), custom_call_target="tpu_custom_call" | custom-call | tf_op jit(solution)/shard_map/pallas_call | solution.py:624
  109.8 1.6 %copy.16 = bf16[128,512]{1,0:T(8,128)(2,1)} copy(bf16[128,512]{1,0:T(8,128)(2,1)} %shard_map.119) | data formatting | bytes 262144
  (1 shorter events, 0.0 us)

commit v2 on v1

--- a/solution.py
+++ b/solution.py
@@ -222,20 +222,6 @@
         k = c * 2 // per_key
         kv_part[c, :, :HD] = keyval[:, k * HD : (k + 1) * HD]
         kv_part[c, :, HD:] = keyval[:, (KVH + k) * HD : (KVH + k + 1) * HD]
-    kv_sends = []
-    for off in range(1, chips):
-        there = lax.rem(chip + off, chips)
-        copy = remote(
-            kv_part.at[there],
-            kv_land.at[chip],
-            k_send.at[off],
-            k_recv.at[chip],
-            wide,
-            there * 2 + core,
-        )
-        copy.start()
-        kv_sends.append(copy)
-
     load.wait()
     total = jnp.zeros((tokens, per_head * HD), jnp.float32)
     for j in range(narrow_count):
@@ -248,27 +234,41 @@
         one = rms_norm(total[:, h * HD : (h + 1) * HD], query_gain_ref[...]).astype(jnp.bfloat16)
         q_all[me, :, h * DRAFT : (h + 1) * DRAFT, :] = one.reshape(requests, DRAFT, HD)
 
-    def exchange_kv():
-        summed = kv_part[chip]
+    kv_sends = []
+
+    def send_kv():
         for off in range(1, chips):
-            there = lax.rem(chip - off + chips, chips)
-            remote(
-                kv_land.at[there],
-                kv_land.at[there],
-                k_send.at[0],
-                k_recv.at[there],
+            there = lax.rem(chip + off, chips)
+            copy = remote(
+                kv_part.at[there],
+                kv_land.at[chip],
+                k_send.at[off],
+                k_recv.at[chip],
                 wide,
                 there * 2 + core,
-            ).wait_recv()
-            summed = summed + kv_land[there]
-        kv_pair[0] = summed
-        copy = remote(
-            kv_pair.at[0], kv_pair.at[1], k_send.at[0], k_recv.at[chips], wide, mate
-        )
-        copy.start()
-        kv_sends.append(copy)
-
-    gather_chips(q_all, q_send, q_recv, wide, me, chips, exchange_kv)
+            )
+            copy.start()
+            kv_sends.append(copy)
+
+    gather_chips(q_all, q_send, q_recv, wide, me, chips, send_kv)
+    summed = kv_part[chip]
+    for off in range(1, chips):
+        there = lax.rem(chip - off + chips, chips)
+        remote(
+            kv_land.at[there],
+            kv_land.at[there],
+            k_send.at[0],
+            k_recv.at[there],
+            wide,
+            there * 2 + core,
+        ).wait_recv()
+        summed = summed + kv_land[there]
+    kv_pair[0] = summed
+    copy = remote(
+        kv_pair.at[0], kv_pair.at[1], k_send.at[0], k_recv.at[chips], wide, mate
+    )
+    copy.start()
+    kv_sends.append(copy)
     q_out[...] = q_all[...]
     remote(
         kv_pair.at[0], kv_pair.at[1], k_send.at[0], k_recv.at[chips], wide, mate

time: 112 us -> 113 us (level)
  no operation moved by 1% of the time
where the time goes in v2:
time: 113 us; the launch traced here: 112 us
  Pallas kernels  109 us (96%)
  local copies, waits for them, and re-layouts  2.39 us (2%)
    pallas_call x1, Pallas kernels, local(): pl.pallas_call(functools.partial(back_kernel, wide_count, narrow_count),...  67 us
    pallas_call x1, Pallas kernels, local(): pl.pallas_call(functools.partial(front_kernel, wide_count, narrow_count),...  42.2 us

profile of v2, /device:TPU:0, one launch (start us, length us, event | category | flops | bytes accessed | tf_op | source)
XLA Modules:
  0.0 112.4 jit_solution(6201424050142088568)
XLA Ops:
  0.0 0.8 convert_element_type.10
  0.8 0.1 copy.13
  0.9 0.7 copy.14.mask_hbm
  1.7 42.2 %shard_map.118 = (bf16[8,8,128,128]{3,2,1,0:T(8,128)(2,1)}, bf16[128,128]{1,0:T(8,128)(2,1)}, f32[128,256]{1,0:T(8,128)}) custom-call(s32[8]{0:T(128)} %owner_ref.3, bf16[128,512]{1,0:T(8,128)(2,1)} %hidden_hbm.1, bf16[128,128]{1,0:T(8,128)(2,1)} %copy.14.mask_hbm, f32[8,1,512]{2,1,0:T(1,128)} %bitcast.7, f32[1,128]{1,0:T(1,128)} %bitcast.8, ...), custom_call_target="tpu_custom_call" | custom-call | tf_op jit(solution)/shard_map/pallas_call | solution.py:577
  43.8 67.0 %shard_map.119 = bf16[128,512]{1,0:T(8,128)(2,1)} custom-call(s32[8]{0:T(128)} %owner_ref.3, s32[8]{0:T(128)} %lengths_ref.1, bf16[8,8,128,128]{3,2,1,0:T(8,128)(2,1)} %get-tuple-element.8.q_ref, bf16[128,128]{1,0:T(8,128)(2,1)} %get-tuple-element.9.mask_ref, f32[128,256]{1,0:T(8,128)} %get-tuple-element.10.kv_ref, f32[1,128]{1,0:T(1,128)} %bitcast.9, ...), custom_call_target="tpu_custom_call" | custom-call | tf_op jit(solution)/shard_map/pallas_call | solution.py:624
  110.9 1.6 %copy.16 = bf16[128,512]{1,0:T(8,128)(2,1)} copy(bf16[128,512]{1,0:T(8,128)(2,1)} %shard_map.119) | data formatting | bytes 262144
  (1 shorter events, 0.0 us)
